TPU v7x, 32 devices: a whole 2x2x4 slice. The times are simulated.
32 devices in a mesh: tri: 8 (over z, y), vir: 4 (over x, core).
Axes of the slice: x: 2, y: 2, z: 4, core: 2. Of those that a mesh axis runs over, the one named last changes fastest.
Arguments:
- amps: bfloat16 [24, 768, 768], P('tri', 'vir'), may hold values from -0.21875 to 0.21875
- vvvo: bfloat16 [24, 768, 128], P('tri', 'vir'), may hold values from -6 to 6
- occ_gap: float32 [16], replicated, may hold values from 0.3 to 1
- vir_gap: float32 [768], P('vir'), may hold values from 0.5 to 2
- pair_gap: float32 [128], replicated, may hold values from 0.5 to 2
- block_sizes: int32 [8], replicated, may hold values from 1 to 3, 16 in all
- roots: int32 [8], replicated, may hold values from 0 to 7, each once
- triples: int32 [96, 2], P('tri'), may hold values from 0 to 7
Outputs:
- density: float32 [768, 128], P('vir')
- grad: float32 [24, 768, 128], P('tri', 'vir')
Inputs may be any that keep to these rules, and one draw needn't show every extreme that they name: `block_sizes`: block sizes sum to 16; at least one block has exactly 3 orbitals. `roots`: each tri index stores exactly one block. `triples`: block numbers; a pair may repeat a block.
All inputs are finite; a program needn't handle non-finite values.
Results may differ from a plain program's by a relative error of at most 0.0003.
Values may be sent and summed in bfloat16 or wider, within the bound.
A program may use at most 128 MiB of HBM per device.

v0:
```python
import jax
import jax.numpy as jnp
from jax import lax
from jax.sharding import PartitionSpec as P

BMAX = 3


def body(amps, vvvo, occ_gap, vir_gap, pair_gap, block_sizes, roots, triples):
    tri_count = lax.axis_size("tri")
    my_index = lax.axis_index("tri")
    pair_count = triples.shape[0]
    vir_local = amps.shape[1]
    vir_count = amps.shape[2]
    pair_width = vvvo.shape[2]
    occ_count = occ_gap.shape[0]
    slot_ids = jnp.arange(BMAX, dtype=jnp.int32)
    blocks = jnp.arange(tri_count, dtype=jnp.int32)
    occ_index = jnp.arange(occ_count, dtype=jnp.int32)
    offsets = jnp.cumsum(block_sizes) - block_sizes
    own_mask = roots == my_index
    own_size = jnp.sum(jnp.where(own_mask, block_sizes, 0))
    own_off = jnp.sum(jnp.where(own_mask, offsets, 0))
    chooser = triples[:, :, None] == blocks
    pair_root = jnp.sum(jnp.where(chooser, roots, 0), axis=2)
    pair_size = jnp.sum(jnp.where(chooser, block_sizes, 0), axis=2)
    pair_off = jnp.sum(jnp.where(chooser, offsets, 0), axis=2)
    row_ids = pair_root[:, :, None] * BMAX + slot_ids

    def energies(first_slot):
        clipped = jnp.minimum(first_slot, occ_count - 1)
        return jnp.sum(jnp.where(clipped[..., None] == occ_index, occ_gap, 0.0), axis=-1)

    pair_gaps = energies(pair_off[:, :, None] + slot_ids)
    own_gaps = energies(own_off + slot_ids)
    pair_live = slot_ids < pair_size[:, :, None]
    own_live = slot_ids < own_size
    everything = lax.all_gather(amps, "tri", axis=0, tiled=True)
    chosen = jnp.take(everything, row_ids.reshape(-1), axis=0).reshape(
        pair_count, 2, BMAX, vir_local, vir_count
    )
    complete_integral_table = lax.all_gather(vvvo, "vir", axis=1, tiled=True)
    base_den = vir_gap[:, None, None] + own_gaps[None, :, None] + pair_gap[None, None, :]

    def pair_terms(picked_pair, left_proj, right_proj, gap_values, live_mask):
        full_den = (
            base_den[None, None]
            + gap_values[0][:, None, None, None, None]
            + gap_values[1][None, :, None, None, None]
        )
        all_live = (
            live_mask[0][:, None, None, None, None]
            & live_mask[1][None, :, None, None, None]
            & own_live[None, None, None, :, None]
        )
        weighted = jnp.where(all_live, left_proj[:, None] * right_proj[None] / full_den, 0.0)
        dens_term = jnp.sum(weighted * weighted, axis=(0, 1, 3))
        left_rows = picked_pair[0].astype(jnp.float32)
        grad_term = jnp.einsum(
            "rnw,rqnhe->hwe", left_rows, weighted, precision=lax.Precision.HIGHEST
        )
        return (dens_term, grad_term)

    start_state = (
        jnp.zeros((vir_local, pair_width), jnp.float32),
        jnp.zeros((BMAX, vir_count, pair_width), jnp.float32),
    )

    def accumulate(state, inputs):
        picked_pair, gap_values, live_mask = inputs
        stacked_rows = picked_pair.reshape(-1, vir_count)
        projected = jnp.einsum(
            "rd,kdm->rkm", stacked_rows, complete_integral_table, preferred_element_type=jnp.float32
        )
        projected = projected.reshape(2, BMAX, vir_local, BMAX, pair_width)
        dens_term, grad_term = pair_terms(
            picked_pair, projected[0], projected[1], gap_values, live_mask
        )
        return ((state[0] + dens_term, state[1] + grad_term), None)

    (density, grad_part), _ = lax.scan(accumulate, start_state, (chosen, pair_gaps, pair_live))
    grad_share = lax.psum_scatter(grad_part, "vir", scatter_dimension=1, tiled=True)
    density_all = lax.psum(density, "tri") / float(tri_count * pair_count)
    return (density_all, grad_share)


def solution(mesh):
    return jax.shard_map(
        body,
        mesh=mesh,
        in_specs=(
            P("tri", "vir", None),
            P("tri", "vir", None),
            P(),
            P("vir"),
            P(),
            P(),
            P(),
            P("tri", None),
        ),
        out_specs=(P("vir", None), P("tri", "vir", None)),
        check_vma=False,
    )
```

profile of v0, /device:TPU:0, one launch (start us, length us, event | category | flops | bytes accessed | tf_op | source)
XLA Modules:
  0.0 349.1 jit_solution(18104560916796286649)
XLA Ops:
  8.8 1.3 fusion.9
  11.3 0.9 fusion.7
  13.1 0.8 select_reduce_fusion.3
  14.0 9.2 %all_gather.7 = bf16[3,768,128]{2,1,0:T(8,128)(2,1)S(1)} all-gather(bf16[3,192,128]{2,1,0:T(8,128)(2,1)} %param.11), channel_id=1, replica_groups=mesh['tri'=8,'vir'=4] {'vir'}, dimensions={1}, use_global_device_ids=true | all-gather | bytes 737280 | tf_op jit(solution)/shard_map/all_gather | solution.py:42
  24.1 97.6 %all-gather.2.cloned.1.call-done = bf16[24,192,768]{2,1,0:T(8,128)(2,1)} async-done(((bf16[3,192,768]{2,1,0:T(8,128)(2,1)}), bf16[24,192,768]{2,1,0:T(8,128)(2,1)}) %all-gather.2.cloned.1.call-update) | async-done | bytes 7077904 | tf_op jit(solution)/shard_map/all_gather | solution.py:38
  121.7 12.1 %gather_fusion = bf16[72,192,768]{2,1,0:T(8,128)(2,1)} fusion(bf16[24,192,768]{2,1,0:T(8,128)(2,1)} %all-gather.2.cloned.1.call-done, s32[1024]{0:T(1024)S(1)} %pad_clamp_fusion), kind=kCustom, calls=%fused_computation | custom fusion | bytes 42467616 | tf_op jit(solution)/shard_map/jit(_take)/gather | solution.py:39
  133.8 15.4 %broadcast_select_fusion = bf16[12,2,3,192,768]{4,3,2,1,0:T(8,128)(2,1)} fusion(bf16[12,2,3,192,768]{4,3,2,1,0:T(8,128)(2,1)} %bitcast.58, pred[12,2,3]{2,1,0:T(4,128)(4,1)S(1)} %compare_and_fusion), kind=kLoop, calls=%fused_computation.23 | loop fusion | flops 10616832 | bytes 42467400 | tf_op jit(solution)/shard_map/jit(_take)/select_n | solution.py:39
  149.2 97.0 %while.13 = (s32[]{:T(128)}, f32[192,128]{1,0:T(8,128)S(1)}, f32[3,768,128]{1,2,0:T(8,128)S(1)}, pred[12,2,3]{2,1,0:T(4,128)(4,1)S(1)}, bf16[12,2,3,192,768]{4,3...) while((s32[]{:T(128)}, f32[192,128]{1,0:T(8,128)S(1)}, ...), condition=%wide.region_11.12_spmd.clone, body=%wide.region_8.11_spmd.clone.sunk | while | flops 2723241984 | bytes 20745844 | solution.py:81
  150.0 1.6 constant_dynamic-slice_fusion.8
  151.6 1.1 fusion.32
  154.0 3.3 fusion.35
  158.1 1.6 constant_dynamic-slice_fusion.8
  159.7 1.1 fusion.32
  162.1 3.3 fusion.35
  166.2 1.6 constant_dynamic-slice_fusion.8
  167.8 1.1 fusion.32
  170.2 3.3 fusion.35
  174.3 1.6 constant_dynamic-slice_fusion.8
  175.9 1.1 fusion.32
  178.2 3.3 fusion.35
  182.4 1.6 constant_dynamic-slice_fusion.8
  184.0 1.1 fusion.32
  186.3 3.3 fusion.35
  190.5 1.6 constant_dynamic-slice_fusion.8
  192.1 1.1 fusion.32
  194.4 3.3 fusion.35
  198.6 1.6 constant_dynamic-slice_fusion.8
  200.2 1.1 fusion.32
  202.5 3.3 fusion.35
  206.6 1.6 constant_dynamic-slice_fusion.8
  208.2 1.1 fusion.32
  210.6 3.3 fusion.35
  214.7 1.6 constant_dynamic-slice_fusion.8
  216.3 1.1 fusion.32
  218.7 3.3 fusion.35
  222.8 1.6 constant_dynamic-slice_fusion.8
  224.4 1.1 fusion.32
  226.8 3.3 fusion.35
  230.9 1.6 constant_dynamic-slice_fusion.8
  232.5 1.1 fusion.32
  234.9 3.3 fusion.35
  239.0 1.6 constant_dynamic-slice_fusion.8
  240.6 1.1 fusion.32
  243.0 3.3 fusion.35
  247.0 1.4 copy.32
  248.4 66.3 %all-reduce.2.cloned.1.call-done = f32[192,128]{1,0:T(8,128)} async-done(((f32[192,128]{1,0:T(8,128)}), f32[192,128]{1,0:T(8,128)}) %all-reduce.2.cloned.1.call-update) | async-done | bytes 98320 | tf_op jit(solution)/shard_map/psum | solution.py:83
  314.7 1.5 broadcast_multiply_fusion
  316.2 26.4 %reduce-scatter.2.cloned.1.call-done = f32[3,192,128]{2,1,0:T(8,128)} async-done(((f32[3,768,128]{2,1,0:T(8,128)}), f32[3,192,128]{2,1,0:T(8,128)}) %reduce-scatter.2.cloned.1.call-update) | async-done | bytes 294928 | tf_op jit(solution)/shard_map/reduce_scatter | solution.py:82
  (172 shorter events, 29.8 us)
Async XLA Ops:
  7.2 114.6 %all-gather.2.cloned.1.call-start = ((), (), s32[]{:S(2)}) async-start(), calls=%async_computation.1 | async-start | bytes 7962624 | tf_op jit(solution)/shard_map/all_gather | solution.py:38
  7.9 306.8 %all-reduce.2.cloned.1.call-start = ((), (), s32[]{:S(2)}) async-start(), calls=%async_computation.2 | async-start | bytes 196608 | tf_op jit(solution)/shard_map/psum | solution.py:83
  133.8 15.4 %copy-start.1 = (f32[128]{0:T(128)S(1)}, f32[128]{0:T(128)}, u32[]{:S(2)}) copy-start(f32[128]{0:T(128)} %param.14) | copy-start | bytes 1540
  246.3 0.6 copy-start
  246.9 95.7 %reduce-scatter.2.cloned.1.call-start = ((), (), s32[]{:S(2)}) async-start(), calls=%async_computation.3 | async-start | bytes 1474560 | tf_op jit(solution)/shard_map/reduce_scatter | solution.py:82
Sparse Core Ops, SparseCore 0:
  10.2 111.4 all-gather.1
  247.0 67.5 all-reduce.1
  317.8 24.7 reduce-scatter.1
where the time goes:
time: 350 us; the launch traced here: 349 us
  waiting for transfers between devices  191 us (55%)
  matrix products  52.2 us (15%)
  other arithmetic  46 us (13%)
  local copies, waits for them, and re-layouts  35.5 us (10%)
  between operations  13.8 us (4%)
  blocking collectives  9.18 us (3%)
    all_gather x1, waiting for transfers between devices, body(): everything = lax.all_gather(amps, 'tri', axis=0, tiled=True)  97.6 us
    psum x1, waiting for transfers between devices, body(): density_all = lax.psum(density, 'tri') / float(tri_count * pair_count)  66.3 us
    dot_general x12, matrix products, pair_terms(): jnp.einsum('rnw,rqnhe->hwe', left_rows, weighted, precision=lax.Precision...  39.1 us
    reduce_scatter x1, waiting for transfers between devices, body(): lax.psum_scatter(grad_part, 'vir', scatter_dimension=1, tiled=True)  26.4 us
    dynamic_slice x36, local copies, waits for them, and re-layouts, body(): lax.scan(accumulate, start_state, (chosen, pair_gaps, pair_live))  19.3 us
    select_n x2, other arithmetic, body(): jnp.take(everything, row_ids.reshape(-1), axis=0)  15.4 us
    dot_general x12, matrix products, accumulate(): jnp.einsum('rd,kdm->rkm', stacked_rows, complete_integral_table, preferre...  13.1 us
    gather x1, local copies, waits for them, and re-layouts, body(): jnp.take(everything, row_ids.reshape(-1), axis=0)  12.1 us
  transfers between devices with their start and end apart: 3, of which 3 were waited for; matrix products, arithmetic and copies ran while one was open for 3% of the time, Pallas kernels for 0%

commit v1 on v0

v1 whole, which is shorter than its diff:
```python
import functools

import jax
import jax.numpy as jnp
from jax import lax
from jax.experimental import pallas as pl
from jax.experimental.pallas import tpu as pltpu
from jax.sharding import PartitionSpec as P

BMAX = 3
MESH = pl.DeviceIdType.MESH


def gather_kernel(tri, vir, amps, vvvo, amps_all, vvvo_all, send_sem, recv_sem, vsend_sem, vrecv_sem, own_sem):
    t = lax.axis_index("tri")
    v = lax.axis_index("vir")
    depth = vvvo.shape[1]
    columns = amps.shape[2] // 2
    odd = t % 2
    place = odd * (tri - 1 - t // 2) + (1 - odd) * (t // 2)

    def owner_at(where):
        where = where % tri
        back = where // (tri // 2)
        return (1 - back) * 2 * where + back * (2 * (tri - 1 - where) + 1)

    toward = (owner_at(place + 1), owner_at(place + tri - 1))

    barrier = pltpu.get_barrier_semaphore()
    for other in toward:
        pl.semaphore_signal(barrier, inc=1, device_id=(other, v), device_id_type=MESH)
    for hop in range(1, vir):
        pl.semaphore_signal(barrier, inc=1, device_id=(t, (v + hop) % vir), device_id_type=MESH)
    pl.semaphore_wait(barrier, 2 + vir - 1)

    def ring_copy(way, step, slot, first):
        source = owner_at(place + tri - step) if way == 0 else owner_at(place + step)
        cols = pl.ds(way * columns, columns)
        landing = amps_all.at[source * BMAX + slot, :, cols]
        return pltpu.make_async_remote_copy(
            src_ref=amps.at[slot, :, cols] if first else landing,
            dst_ref=landing,
            send_sem=send_sem.at[way, step, slot],
            recv_sem=recv_sem.at[way, step, slot],
            device_id=(toward[way], v),
            device_id_type=MESH,
        )

    def arrival(way, step, slot):
        source = owner_at(place + tri - step - 1) if way == 0 else owner_at(place + step + 1)
        landing = amps_all.at[source * BMAX + slot, :, pl.ds(way * columns, columns)]
        return pltpu.make_async_remote_copy(
            src_ref=landing,
            dst_ref=landing,
            send_sem=send_sem.at[way, step, slot],
            recv_sem=recv_sem.at[way, step, slot],
            device_id=(toward[way], v),
            device_id_type=MESH,
        )

    pieces = [(slot, way) for slot in range(BMAX) for way in range(2)]
    for slot, way in pieces:
        ring_copy(way, 0, slot, True).start()

    def integral_copy(hop, holder, target):
        return pltpu.make_async_remote_copy(
            src_ref=vvvo,
            dst_ref=vvvo_all.at[:, pl.ds(holder * depth, depth), :],
            send_sem=vsend_sem.at[hop - 1],
            recv_sem=vrecv_sem.at[hop - 1],
            device_id=(t, target),
            device_id_type=MESH,
        )

    for hop in range(1, vir):
        integral_copy(hop, v, (v + hop) % vir).start()
    own_amps = pltpu.make_async_copy(amps, amps_all.at[pl.ds(t * BMAX, BMAX)], own_sem.at[0])
    own_vvvo = pltpu.make_async_copy(vvvo, vvvo_all.at[:, pl.ds(v * depth, depth), :], own_sem.at[1])
    own_amps.start()
    own_vvvo.start()

    def forward(step, carry):
        for slot, way in pieces:
            arrival(way, step - 1, slot).wait_recv()
            ring_copy(way, step, slot, False).start()
        return carry

    lax.fori_loop(1, tri - 1, forward, 0)
    for slot, way in pieces:
        arrival(way, tri - 2, slot).wait_recv()
    for slot, way in pieces:
        ring_copy(way, 0, slot, True).wait_send()

    def drain(step, carry):
        for slot, way in pieces:
            ring_copy(way, step, slot, False).wait_send()
        return carry

    lax.fori_loop(1, tri - 1, drain, 0)
    for hop in range(1, vir):
        integral_copy(hop, (v + vir - hop) % vir, (v + hop) % vir).wait_recv()
        integral_copy(hop, v, (v + hop) % vir).wait_send()
    own_amps.wait()
    own_vvvo.wait()


def contract_kernel(
    sizes, roots, triples, occ_gap, vir_gap, pair_gap, amps, vvvo,
    density, grad, offsets, used, proj, weights, base, total,
):
    tri = sizes.shape[0]
    pairs = triples.shape[0]
    occ_count = occ_gap.shape[0]
    rows = amps.shape[1]
    width = vvvo.shape[2]
    t = lax.axis_index("tri")

    def walk(b, carry):
        start, own = carry
        offsets[b] = start
        used[roots[b]] = 0
        return start + sizes[b], jnp.where(roots[b] == t, b, own)

    _, own = lax.fori_loop(0, tri, walk, (jnp.int32(0), jnp.int32(0)))
    own_size = sizes[own]

    def gap(b, slot):
        return occ_gap[jnp.minimum(offsets[b] + slot, occ_count - 1)]

    outer = vir_gap[...] + pair_gap[...]
    for k in range(BMAX):
        base[k] = outer + gap(own, k)

    table = jnp.concatenate([vvvo[k] for k in range(BMAX)], axis=1)

    def project(b, carry):
        def one(slot, inner):
            row = roots[b] * BMAX + slot
            product = jnp.dot(amps[row], table, preferred_element_type=jnp.float32)
            for k in range(BMAX):
                proj[row, k] = product[:, k * width:(k + 1) * width]
            return inner

        return lax.fori_loop(0, sizes[b], one, carry)

    lax.fori_loop(0, tri, project, 0)
    density[...] = jnp.zeros_like(density)
    total[...] = jnp.zeros_like(total)

    def mark(q, carry):
        left_root = roots[triples[q, 0]]

        @pl.when(used[left_root] == 0)
        def _():
            used[left_root] = 1
            for slot in range(BMAX):
                weights[left_root * BMAX + slot] = jnp.zeros(weights.shape[1:], jnp.float32)

        return carry

    lax.fori_loop(0, pairs, mark, 0)
    tile = 48
    scale = 1.0 / float(tri * pairs)

    def one_pair(q, carry):
        left, right = triples[q, 0], triples[q, 1]
        left_row, right_row = roots[left] * BMAX, roots[right] * BMAX
        for count in range(1, BMAX + 1):

            @pl.when(sizes[right] == count)
            def _():
                right_gaps = [gap(right, j) for j in range(count)]

                def one_k(k, inner):
                    def one_left(i, deepest):
                        row = left_row + i
                        left_gap = gap(left, i)
                        for first in range(0, rows, tile):
                            at = pl.ds(first, tile)
                            p = proj[row, k, at, :]
                            den = base[k, at, :]
                            squares = density[at, :]
                            summed = weights[row, k, at, :]
                            for j in range(count):
                                d = den + (left_gap + right_gaps[j])
                                r = pl.reciprocal(d, approx=True)
                                r = r * (2.0 - d * r)
                                y = p * proj[right_row + j, k, at, :] * r
                                squares = squares + y * y
                                summed = summed + y
                            density[at, :] = squares
                            weights[row, k, at, :] = summed
                        return deepest

                    return lax.fori_loop(0, sizes[left], one_left, inner)

                lax.fori_loop(0, own_size, one_k, 0)

        return carry

    lax.fori_loop(0, pairs, one_pair, 0)
    density[...] = density[...] * scale

    def contract(b, carry):
        @pl.when(used[b] == 1)
        def _():
            stacked = amps[pl.ds(b * BMAX, BMAX)].reshape(BMAX * rows, amps.shape[2])
            high, low = [], []
            for k in range(BMAX):
                w = weights[pl.ds(b * BMAX, BMAX), k].reshape(BMAX * rows, width)
                top = w.astype(jnp.bfloat16)
                high.append(top)
                low.append((w - top.astype(jnp.float32)).astype(jnp.bfloat16))
            total[...] += lax.dot_general(
                stacked,
                jnp.concatenate(high + low, axis=1),
                (((0,), (0,)), ((), ())),
                preferred_element_type=jnp.float32,
            )

        return carry

    lax.fori_loop(0, tri, contract, 0)
    for k in range(BMAX):
        upper = total[:, k * width:(k + 1) * width]
        lower = total[:, (BMAX + k) * width:(BMAX + k + 1) * width]
        grad[k] = upper + lower


def reduce_kernel(tri, vir, grad, dens, grad_out, dens_out, grad_in, dens_in, gsend, grecv, dsend, drecv):
    t = lax.axis_index("tri")
    v = lax.axis_index("vir")
    depth = grad_out.shape[1]
    steps = tri.bit_length() - 1

    def partner(step):
        far = 1 << step
        bit = (t // far) % 2
        return t + far * (1 - 2 * bit)

    barrier = pltpu.get_barrier_semaphore()
    for hop in range(1, vir):
        pl.semaphore_signal(barrier, inc=1, device_id=(t, (v + hop) % vir), device_id_type=MESH)
    for step in range(steps):
        pl.semaphore_signal(barrier, inc=1, device_id=(partner(step), v), device_id_type=MESH)
    pl.semaphore_wait(barrier, vir - 1 + steps)

    def slice_copy(hop):
        target = (v + hop) % vir
        return pltpu.make_async_remote_copy(
            src_ref=grad.at[:, pl.ds(pl.multiple_of(target * depth, 16), depth), :],
            dst_ref=grad_in.at[hop - 1],
            send_sem=gsend.at[hop - 1],
            recv_sem=grecv.at[hop - 1],
            device_id=(t, target),
            device_id_type=MESH,
        )

    def density_copy(step):
        return pltpu.make_async_remote_copy(
            src_ref=dens if step == 0 else dens_out.at[step - 1],
            dst_ref=dens_in.at[step],
            send_sem=dsend.at[step],
            recv_sem=drecv.at[step],
            device_id=(partner(step), v),
            device_id_type=MESH,
        )

    density_copy(0).start()
    for hop in range(1, vir):
        slice_copy(hop).start()
    held = dens[...]
    for step in range(steps):
        density_copy(step).wait_recv()
        held = held + dens_in[step]
        dens_out[step] = held
        if step + 1 < steps:
            density_copy(step + 1).start()
    grad_out[...] = grad[:, pl.ds(pl.multiple_of(v * depth, 16), depth), :]
    for hop in range(1, vir):
        slice_copy(hop).wait_recv()
        grad_out[...] += grad_in[hop - 1]
    for hop in range(1, vir):
        slice_copy(hop).wait_send()
    for step in range(steps):
        density_copy(step).wait_send()


def body(tri, vir, amps, vvvo, occ_gap, vir_gap, pair_gap, block_sizes, roots, triples):
    rows, full = amps.shape[1:]
    depth, width = vvvo.shape[1:]
    anywhere = pl.BlockSpec(memory_space=pl.ANY)
    in_vmem = pl.BlockSpec(memory_space=pltpu.VMEM)
    in_smem = pl.BlockSpec(memory_space=pltpu.SMEM)
    f32 = jnp.float32
    amps_all, vvvo_all = pl.pallas_call(
        functools.partial(gather_kernel, tri, vir),
        out_shape=(
            jax.ShapeDtypeStruct((tri * BMAX, rows, full), amps.dtype),
            jax.ShapeDtypeStruct((BMAX, full, width), vvvo.dtype),
        ),
        in_specs=[anywhere] * 2,
        out_specs=(anywhere, anywhere),
        scratch_shapes=[
            pltpu.SemaphoreType.DMA((2, tri - 1, BMAX)),
            pltpu.SemaphoreType.DMA((2, tri - 1, BMAX)),
            pltpu.SemaphoreType.DMA((vir - 1,)),
            pltpu.SemaphoreType.DMA((vir - 1,)),
            pltpu.SemaphoreType.DMA((2,)),
        ],
        compiler_params=pltpu.CompilerParams(collective_id=0, has_side_effects=True),
        name="gather_rows",
    )(amps, vvvo)
    density, grad = pl.pallas_call(
        contract_kernel,
        out_shape=(
            jax.ShapeDtypeStruct((rows, width), f32),
            jax.ShapeDtypeStruct((BMAX, full, width), f32),
        ),
        in_specs=[in_smem] * 4 + [in_vmem] * 4,
        out_specs=(in_vmem, in_vmem),
        scratch_shapes=[
            pltpu.SMEM((tri,), jnp.int32),
            pltpu.SMEM((tri,), jnp.int32),
            pltpu.VMEM((tri * BMAX, BMAX, rows, width), f32),
            pltpu.VMEM((tri * BMAX, BMAX, rows, width), f32),
            pltpu.VMEM((BMAX, rows, width), f32),
            pltpu.VMEM((full, 2 * BMAX * width), f32),
        ],
        compiler_params=pltpu.CompilerParams(vmem_limit_bytes=48 << 20),
        name="contract_pairs",
    )(block_sizes, roots, triples, occ_gap, vir_gap[:, None], pair_gap[None, :], amps_all, vvvo_all)
    steps = tri.bit_length() - 1
    grad_share, density_steps = pl.pallas_call(
        functools.partial(reduce_kernel, tri, vir),
        out_shape=(
            jax.ShapeDtypeStruct((BMAX, depth, width), f32),
            jax.ShapeDtypeStruct((steps, rows, width), f32),
        ),
        in_specs=[in_vmem] * 2,
        out_specs=(in_vmem, in_vmem),
        scratch_shapes=[
            pltpu.VMEM((vir - 1, BMAX, depth, width), f32),
            pltpu.VMEM((steps, rows, width), f32),
            pltpu.SemaphoreType.DMA((vir - 1,)),
            pltpu.SemaphoreType.DMA((vir - 1,)),
            pltpu.SemaphoreType.DMA((steps,)),
            pltpu.SemaphoreType.DMA((steps,)),
        ],
        compiler_params=pltpu.CompilerParams(
            collective_id=1, has_side_effects=True, vmem_limit_bytes=16 << 20
        ),
        name="reduce_sums",
    )(grad, density)
    return density_steps[steps - 1], grad_share


def solution(mesh):
    return jax.shard_map(
        functools.partial(body, mesh.shape["tri"], mesh.shape["vir"]),
        mesh=mesh,
        in_specs=(
            P("tri", "vir", None),
            P("tri", "vir", None),
            P(),
            P("vir"),
            P(),
            P(),
            P(),
            P("tri", None),
        ),
        out_specs=(P("vir", None), P("tri", "vir", None)),
        check_vma=False,
    )
```

time: 350 us -> 119 us (0.34)
  waiting for transfers between devices: 191 us -> 0 us
  Pallas kernels: 0 us -> 112 us
  matrix products: 52.2 us -> 0 us
  other arithmetic: 46 us -> 0 us
  local copies, waits for them, and re-layouts: 35.5 us -> 6.59 us
  between operations: 13.8 us -> 0.67 us
  blocking collectives: 9.18 us -> 0 us
    pallas_call x0 -> x3, Pallas kernels: none -> 112 us  [the longest x1 73.2 us: body(): pl.pallas_call(functools.partial(gather_kernel, tri, vir), out_shape=(jax...]
    all_gather x1 -> x0, waiting for transfers between devices: 97.6 us -> none  [body(): everything = lax.all_gather(amps, 'tri', axis=0, tiled=True)]
    psum x1 -> x0, waiting for transfers between devices: 66.3 us -> none  [body(): density_all = lax.psum(density, 'tri') / float(tri_count * pair_count)]
    dot_general x24 -> x0, matrix products: 52.2 us -> none  [the longest x12 39.1 us: pair_terms(): jnp.einsum('rnw,rqnhe->hwe', left_rows, weighted, precision=lax.Precision...]
    reduce_scatter x1 -> x0, waiting for transfers between devices: 26.4 us -> none  [body(): lax.psum_scatter(grad_part, 'vir', scatter_dimension=1, tiled=True)]
    dynamic_slice x36 -> x0, local copies, waits for them, and re-layouts: 19.3 us -> none  [body(): lax.scan(accumulate, start_state, (chosen, pair_gaps, pair_live))]
    select_n x2 -> x0, other arithmetic: 15.4 us -> none  [body(): jnp.take(everything, row_ids.reshape(-1), axis=0)]
    reduce_sum x16 -> x0, other arithmetic: 13.5 us -> none  [the longest x12 9.7 us: pair_terms(): jnp.einsum('rnw,rqnhe->hwe', left_rows, weighted, precision=lax.Precision...]
  transfers between devices with their start and end apart: 3 -> 0, of which waited for: 3 -> 0; matrix products, arithmetic and copies ran while one was open for 3% -> 0% of each run, Pallas kernels for 0% -> 0%
where the time goes in v1:
time: 119 us
  Pallas kernels  112 us (94%)
  local copies, waits for them, and re-layouts  6.59 us (6%)
    pallas_call x1, Pallas kernels, body(): pl.pallas_call(functools.partial(gather_kernel, tri, vir), out_shape=(jax...  73.2 us
    pallas_call x1, Pallas kernels, body(): pl.pallas_call(contract_kernel, out_shape=(jax.ShapeDtypeStruct((rows, wi...  24.6 us
    pallas_call x1, Pallas kernels, body(): pl.pallas_call(functools.partial(reduce_kernel, tri, vir), out_shape=(jax...  14.3 us
    unnamed x12, local copies, waits for them, and re-layouts  5.16 us

profile of v1, /device:TPU:0, one launch (start us, length us, event | category | flops | bytes accessed | tf_op | source)
XLA Modules:
  0.0 119.3 jit_solution(13359276632206841844)
XLA Ops:
  0.6 0.8 copy.11.triples
  1.4 0.8 copy.12.vir_gap
  2.2 73.2 %gather_rows.1 = (bf16[24,192,768]{2,1,0:T(8,128)(2,1)}, bf16[3,768,128]{2,1,0:T(8,128)(2,1)}) custom-call(bf16[3,192,768]{2,1,0:T(8,128)(2,1)} %amps.1, bf16[3,192,128]{2,1,0:T(8,128)(2,1)} %vvvo.1), custom_call_target="tpu_custom_call" | custom-call | tf_op jit(solution)/shard_map/gather_rows/pallas_call | solution.py:296
  75.4 0.0 copy-start
  75.4 1.1 copy-done
  76.4 0.0 copy-start.1
  76.4 0.7 copy-done.1
  77.1 0.0 copy-start.2
  77.1 0.7 copy-done.2
  77.7 0.0 copy-start.3
  77.7 0.7 copy-done.3
  78.4 0.0 copy-start.4
  78.4 0.7 copy-done.4
  79.1 24.6 %contract_pairs.1 = (f32[192,128]{1,0:T(8,128)S(1)}, f32[3,768,128]{2,1,0:T(8,128)S(1)}) custom-call(s32[8]{0:T(128)S(1)} %copy-done.1, s32[8]{0:T(128)S(1)} %copy-done.2, s32[12,2]{1,0:T(8,128)S(1)} %copy.11.triples, f32[16]{0:T(128)S(1)} %copy-done.3, f32[192,1]{1,0:T(8,128)S(1)} %copy.12.vir_gap, f32[1,128]{1,0:T(1,128)S(1)} %bitcast.4, ...), custom_call_target="tpu_custom_call" | custom-call | tf_op jit(solution)/shard_map/contract_pairs/pallas_call | solution.py:314
  103.6 14.3 %reduce_sums.1 = (f32[3,192,128]{2,1,0:T(8,128)S(1)}, f32[3,192,128]{2,1,0:T(8,128)S(1)}) custom-call(f32[3,768,128]{2,1,0:T(8,128)S(1)} %get-tuple-element.10.grad, f32[192,128]{1,0:T(8,128)S(1)} %get-tuple-element.11.dens), custom_call_target="tpu_custom_call" | custom-call | tf_op jit(solution)/shard_map/reduce_sums/pallas_call | solution.py:334
  117.9 0.6 slice_bitcast_fusion
  118.6 0.7 copy.14
Async XLA Ops:
  75.4 1.1 copy-start
  76.4 0.7 copy-start.1
  77.1 0.7 copy-start.2
  77.7 0.7 copy-start.3
  78.4 0.7 copy-start.4

commit v2 on v0

v2 whole, which is shorter than its diff:
```python
import functools

import jax
import jax.numpy as jnp
from jax import lax
from jax.experimental import pallas as pl
from jax.experimental.pallas import tpu as pltpu
from jax.sharding import PartitionSpec as P

BMAX = 3
MESH = pl.DeviceIdType.MESH


def bits_of(count):
    return count.bit_length() - 1


def gather_kernel(
    tri, vir, split, amps, vvvo, triples, amps_all, vvvo_all, triples_all,
    send_sem, recv_sem, psend_sem, precv_sem, vsend_sem, vrecv_sem, xsend_sem, xrecv_sem, own_sem,
):
    t = lax.axis_index("tri")
    v = lax.axis_index("vir")
    ring = tri // split
    part = t // ring
    member = t % ring
    other_owner = (t + ring) % tri
    depth = vvvo.shape[1]
    rows = amps.shape[1] // split
    columns = amps.shape[2] // 2
    odd = member % 2
    place = odd * (ring - 1 - member // 2) + (1 - odd) * (member // 2)

    def member_at(where):
        where = where % ring
        back = where // (ring // 2)
        return (1 - back) * 2 * where + back * (2 * (ring - 1 - where) + 1)

    toward = tuple(part * ring + member_at(place + step) for step in (1, ring - 1))

    barrier = pltpu.get_barrier_semaphore()
    for other in toward:
        pl.semaphore_signal(barrier, inc=1, device_id=(other, v), device_id_type=MESH)
    for hop in range(1, vir):
        pl.semaphore_signal(barrier, inc=1, device_id=(t, (v + hop) % vir), device_id_type=MESH)
    if split == 2:
        pl.semaphore_signal(barrier, inc=1, device_id=(other_owner, v), device_id_type=MESH)
    pl.semaphore_wait(barrier, 2 + vir - 1 + split - 1)

    def part_rows(which):
        return pl.ds(pl.multiple_of(which * rows, 16), rows)

    def ring_copy(e, way, step, slot, arriving=False, first=False):
        shift = step + 1 if arriving else step
        source = member_at(place + ring - shift) if way == 0 else member_at(place + shift)
        half = (part + e) % split
        cols = pl.ds(way * columns, columns)
        landing = amps_all.at[(half * ring + source) * BMAX + slot, :, cols]
        return pltpu.make_async_remote_copy(
            src_ref=amps.at[slot, part_rows(part), cols] if first else landing,
            dst_ref=landing,
            send_sem=send_sem.at[e, way, step, slot],
            recv_sem=recv_sem.at[e, way, step, slot],
            device_id=(toward[way], v),
            device_id_type=MESH,
        )

    def start_ring(e, step, slot):
        for way in range(2):
            ring_copy(e, way, step, slot, first=e == 0).start()

    def forward(e, step, slot):
        for way in range(2):
            ring_copy(e, way, step - 1, slot, arriving=True).wait_recv()
            ring_copy(e, way, step, slot).start()

    def partner_copy(slot, owner):
        return pltpu.make_async_remote_copy(
            src_ref=amps.at[slot, part_rows((part + 1) % split), :],
            dst_ref=amps_all.at[owner * BMAX + slot],
            send_sem=psend_sem.at[slot],
            recv_sem=precv_sem.at[slot],
            device_id=(other_owner, v),
            device_id_type=MESH,
        )

    def to_partner(index, source, landing):
        return pltpu.make_async_remote_copy(
            src_ref=source,
            dst_ref=landing,
            send_sem=xsend_sem.at[index],
            recv_sem=xrecv_sem.at[index],
            device_id=(other_owner, v),
            device_id_type=MESH,
        )

    def integral_place(e, holder):
        at = pl.ds(pl.multiple_of(holder * depth, 16), depth)
        return vvvo_all.at[pl.ds(e * BMAX, BMAX), at, :]

    def integral_copy(e, hop, holder):
        return pltpu.make_async_remote_copy(
            src_ref=vvvo if e == 0 else integral_place(e, v),
            dst_ref=integral_place(e, holder),
            send_sem=vsend_sem.at[e, hop - 1],
            recv_sem=vrecv_sem.at[e, hop - 1],
            device_id=(t, (v + hop) % vir),
            device_id_type=MESH,
        )

    across = []
    if split == 2:
        across = [
            to_partner(0, triples, triples_all.at[1]),
            to_partner(1, vvvo, integral_place(1, v)),
        ]
    for copy in across:
        copy.start()
    for slot in range(BMAX):
        start_ring(0, 0, slot)
        if split == 2:
            partner_copy(slot, t).start()
    for hop in range(1, vir):
        integral_copy(0, hop, v).start()
    own = [
        pltpu.make_async_copy(
            amps.at[:, part_rows(part), :], amps_all.at[pl.ds(t * BMAX, BMAX)], own_sem.at[0]
        ),
        pltpu.make_async_copy(vvvo, integral_place(0, v), own_sem.at[1]),
        pltpu.make_async_copy(triples, triples_all.at[0], own_sem.at[2]),
    ]
    for copy in own:
        copy.start()

    if split == 2:
        for copy in across:
            copy.wait_recv()
        for hop in range(1, vir):
            integral_copy(1, hop, v).start()
        order = [(44 * step + 15 * slot, 0, step, slot) for step in range(1, ring - 1) for slot in range(BMAX)]
        order += [(60 * (slot + 1) + 44 * step, 1, step, slot) for step in range(ring - 1) for slot in range(BMAX)]
        for _, e, step, slot in sorted(order):
            if step == 0:
                partner_copy(slot, other_owner).wait_recv()
                start_ring(1, 0, slot)
            else:
                forward(e, step, slot)
    else:
        def hop_on(step, carry):
            for slot in range(BMAX):
                forward(0, step, slot)
            return carry

        lax.fori_loop(1, ring - 1, hop_on, 0)

    for e in range(split):
        for slot in range(BMAX):
            for way in range(2):
                ring_copy(e, way, ring - 2, slot, arriving=True).wait_recv()
                ring_copy(e, way, 0, slot, first=e == 0).wait_send()

        def drain(step, carry):
            for slot in range(BMAX):
                for way in range(2):
                    ring_copy(e, way, step, slot).wait_send()
            return carry

        lax.fori_loop(1, ring - 1, drain, 0)
        for hop in range(1, vir):
            integral_copy(e, hop, (v + vir - hop) % vir).wait_recv()
            integral_copy(e, hop, v).wait_send()
    if split == 2:
        for copy in across:
            copy.wait_send()
        for slot in range(BMAX):
            partner_copy(slot, t).wait_send()
    for copy in own:
        copy.wait()


def contract_kernel(
    split, tri, sizes, roots, triples, occ_gap, vir_gap, pair_gap, amps, vvvo,
    density, grad, offsets, rows_in, proj, weights, base, row_sem,
):
    pairs = triples.shape[2] // 2
    occ_count = occ_gap.shape[0]
    rows = amps.shape[1]
    width = vvvo.shape[2]
    layers = split * BMAX
    t = lax.axis_index("tri")
    ring = tri // split

    def fetch(b, start):
        offsets[b] = start

        def one(slot, carry):
            pltpu.make_async_copy(
                amps.at[roots[b] * BMAX + slot], rows_in.at[start + slot], row_sem.at[start + slot]
            ).start()
            return carry

        lax.fori_loop(0, sizes[b], one, 0)
        return start + sizes[b]

    lax.fori_loop(0, tri, fetch, jnp.int32(0))

    def find(owner):
        return lax.fori_loop(
            0, tri, lambda b, found: jnp.where(roots[b] == owner, b, found), jnp.int32(0)
        )

    owned = [find((t + e * ring) % tri) for e in range(split)]
    outer = vir_gap[pl.ds(pl.multiple_of((t // ring) * rows, 8), rows), :] + pair_gap[...]
    for e in range(split):
        for k in range(BMAX):
            own_gap = occ_gap[jnp.minimum(offsets[owned[e]] + k, occ_count - 1)]
            base[e * BMAX + k] = outer + own_gap
    density[...] = jnp.zeros_like(density)
    weights[...] = jnp.zeros_like(weights)
    table = jnp.concatenate([vvvo[layer] for layer in range(layers)], axis=1)
    group = 768 // rows
    span = group * rows

    def stacked(g):
        return rows_in[pl.ds(g * group, group)].reshape(span, rows_in.shape[2])

    def project(g, carry):
        for r in range(group):
            o = g * group + r
            pltpu.make_async_copy(amps.at[0], rows_in.at[o], row_sem.at[o]).wait()
        proj[pl.ds(pl.multiple_of(g * span, span), span), :] = jnp.dot(
            stacked(g), table, preferred_element_type=jnp.float32
        )
        return carry

    lax.fori_loop(0, occ_count // group, project, 0)
    tile = 48
    scale = 1.0 / float(tri * pairs)

    def one_pair(e, q):
        left, right = triples[e, 0, 2 * q], triples[e, 0, 2 * q + 1]
        left_first, right_first = offsets[left], offsets[right]
        for count in range(1, BMAX + 1):

            @pl.when(sizes[right] == count)
            def _():
                right_gaps = [occ_gap[right_first + j] for j in range(count)]

                def one_k(k, carry):
                    layer = e * BMAX + k
                    lanes = pl.ds(pl.multiple_of(layer * width, width), width)

                    def one_left(i, inner):
                        o = left_first + i
                        left_gap = occ_gap[o]
                        for first in range(0, rows, tile):
                            at = pl.ds(first, tile)
                            here = pl.ds(pl.multiple_of(o * rows, 8) + first, tile)
                            p = proj[here, lanes]
                            den = base[layer, at, :]
                            squares = density[at, :]
                            summed = weights[here, lanes]
                            for j in range(count):
                                there = pl.ds(pl.multiple_of((right_first + j) * rows, 8) + first, tile)
                                d = den + (left_gap + right_gaps[j])
                                r = pl.reciprocal(d, approx=True)
                                r = r * (2.0 - d * r)
                                y = p * proj[there, lanes] * r
                                squares = squares + y * y
                                summed = summed + y
                            density[at, :] = squares
                            weights[here, lanes] = summed
                        return inner

                    return lax.fori_loop(0, sizes[left], one_left, carry)

                lax.fori_loop(0, sizes[owned[e]], one_k, 0)

    for e in range(split):

        def each(q, carry):
            one_pair(e, q)
            return carry

        lax.fori_loop(0, pairs, each, 0)
    density[...] = density[...] * scale

    def product(g):
        left = stacked(g)
        w = weights[pl.ds(g * span, span), :]
        top = w.astype(jnp.bfloat16)
        rest = (w - top.astype(jnp.float32)).astype(jnp.bfloat16)
        over_rows = (((0,), (0,)), ((), ()))
        return lax.dot_general(
            left, top, over_rows, preferred_element_type=jnp.float32
        ) + lax.dot_general(left, rest, over_rows, preferred_element_type=jnp.float32)

    grad[...] = product(0)
    for g in range(1, occ_count // group):
        grad[...] += product(g)


def reduce_kernel(tri, vir, split, grad, dens, grad_out, dens_out, *scratch):
    levels = bits_of(vir)
    came, sums = scratch[:levels], scratch[levels:2 * levels]
    from_partner, dens_in, dens_sum, gsend, grecv, psend, precv, dsend, drecv = scratch[2 * levels:]
    t = lax.axis_index("tri")
    v = lax.axis_index("vir")
    depth, width = grad_out.shape[1:]
    rows = dens.shape[0]
    ring = tri // split
    steps = bits_of(ring)
    other_owner = (t + ring) % tri
    part = t // ring

    def bit(number, level):
        return (number // (1 << level)) % 2

    def flipped(number, level):
        return number + (1 << level) * (1 - 2 * bit(number, level))

    barrier = pltpu.get_barrier_semaphore()
    for level in range(levels):
        pl.semaphore_signal(barrier, inc=1, device_id=(t, flipped(v, level)), device_id_type=MESH)
    for step in range(steps):
        pl.semaphore_signal(barrier, inc=1, device_id=(flipped(t, step), v), device_id_type=MESH)
    if split == 2:
        pl.semaphore_signal(barrier, inc=1, device_id=(other_owner, v), device_id_type=MESH)
    pl.semaphore_wait(barrier, levels + steps + split - 1)

    def lanes(chunk):
        return pl.ds(chunk * width, width)

    def slab(holder):
        return pl.ds(pl.multiple_of(holder * depth, 16), depth)

    def halving(level, chunk, j):
        away = 2 * j + 1 - bit(v, level)
        return pltpu.make_async_remote_copy(
            src_ref=grad.at[slab(away), lanes(chunk)] if level == 0 else sums[level - 1].at[chunk, away],
            dst_ref=came[level].at[chunk, j],
            send_sem=gsend.at[level, chunk, j],
            recv_sem=grecv.at[level, chunk, j],
            device_id=(t, flipped(v, level)),
            device_id_type=MESH,
        )

    def partner_copy(k):
        return pltpu.make_async_remote_copy(
            src_ref=sums[levels - 1].at[BMAX + k, 0],
            dst_ref=from_partner.at[k],
            send_sem=psend.at[k],
            recv_sem=precv.at[k],
            device_id=(other_owner, v),
            device_id_type=MESH,
        )

    def density_copy(step):
        return pltpu.make_async_remote_copy(
            src_ref=dens if step == 0 else dens_sum.at[step - 1],
            dst_ref=dens_in.at[step],
            send_sem=dsend.at[step],
            recv_sem=drecv.at[step],
            device_id=(flipped(t, step), v),
            device_id_type=MESH,
        )

    def part_copy(which):
        at = pl.ds(pl.multiple_of(which * rows, 8), rows)
        return pltpu.make_async_remote_copy(
            src_ref=dens_out.at[at, :],
            dst_ref=dens_out.at[at, :],
            send_sem=dsend.at[steps],
            recv_sem=drecv.at[steps],
            device_id=(other_owner, v),
            device_id_type=MESH,
        )

    chunks = [e * BMAX + k for e in reversed(range(split)) for k in range(BMAX)]
    for chunk in chunks:
        for j in range(vir // 2):
            halving(0, chunk, j).start()
    density_copy(0).start()
    for level in range(levels):
        if level:
            step = level - 1
            if step < steps:
                density_copy(step).wait_recv()
                dens_sum[step] = (dens[...] if step == 0 else dens_sum[step - 1]) + dens_in[step]
                if step + 1 < steps:
                    density_copy(step + 1).start()
        for chunk in chunks:
            for j in range(vir >> (level + 1)):
                halving(level, chunk, j).wait_recv()
                kept = 2 * j + bit(v, level)
                held = grad[slab(kept), lanes(chunk)] if level == 0 else sums[level - 1][chunk, kept]
                sums[level][chunk, j] = held + came[level][chunk, j]
            if level + 1 < levels:
                for j in range(vir >> (level + 2)):
                    halving(level + 1, chunk, j).start()
            elif chunk >= BMAX:
                partner_copy(chunk - BMAX).start()
    for step in range(max(levels - 1, 0), steps):
        density_copy(step).wait_recv()
        dens_sum[step] = (dens[...] if step == 0 else dens_sum[step - 1]) + dens_in[step]
        if step + 1 < steps:
            density_copy(step + 1).start()
    dens_out[pl.ds(pl.multiple_of(part * rows, 8), rows), :] = dens_sum[steps - 1]
    if split == 2:
        part_copy(part).start()
    for k in range(BMAX):
        if split == 2:
            partner_copy(k).wait_recv()
            grad_out[k] = sums[levels - 1][k, 0] + from_partner[k]
        else:
            grad_out[k] = sums[levels - 1][k, 0]
    for level in range(levels):
        for chunk in chunks:
            for j in range(vir >> (level + 1)):
                halving(level, chunk, j).wait_send()
    for step in range(steps):
        density_copy(step).wait_send()
    if split == 2:
        for k in range(BMAX):
            partner_copy(k).wait_send()
        part_copy(1 - part).wait_recv()
        part_copy(part).wait_send()


def body(tri, vir, amps, vvvo, occ_gap, vir_gap, pair_gap, block_sizes, roots, triples):
    own_rows, full = amps.shape[1:]
    depth, width = vvvo.shape[1:]
    pairs = triples.shape[0]
    occ_count = occ_gap.shape[0]
    split = 2 if own_rows % 32 == 0 and tri % 4 == 0 else 1
    ring = tri // split
    rows = own_rows // split
    layers = split * BMAX
    anywhere = pl.BlockSpec(memory_space=pl.ANY)
    in_vmem = pl.BlockSpec(memory_space=pltpu.VMEM)
    in_smem = pl.BlockSpec(memory_space=pltpu.SMEM)
    f32 = jnp.float32
    dma = pltpu.SemaphoreType.DMA
    amps_all, vvvo_all, triples_all = pl.pallas_call(
        functools.partial(gather_kernel, tri, vir, split),
        out_shape=(
            jax.ShapeDtypeStruct((tri * BMAX, rows, full), amps.dtype),
            jax.ShapeDtypeStruct((layers, full, width), vvvo.dtype),
            jax.ShapeDtypeStruct((split, 1, 2 * pairs), triples.dtype),
        ),
        in_specs=[anywhere] * 3,
        out_specs=(anywhere,) * 3,
        scratch_shapes=[
            dma((split, 2, ring - 1, BMAX)),
            dma((split, 2, ring - 1, BMAX)),
            dma((BMAX,)),
            dma((BMAX,)),
            dma((split, vir - 1)),
            dma((split, vir - 1)),
            dma((2,)),
            dma((2,)),
            dma((3,)),
        ],
        compiler_params=pltpu.CompilerParams(collective_id=0, has_side_effects=True),
        name="gather_rows",
    )(amps, vvvo, triples.reshape(1, 2 * pairs))
    density, grad = pl.pallas_call(
        functools.partial(contract_kernel, split, tri),
        out_shape=(
            jax.ShapeDtypeStruct((rows, width), f32),
            jax.ShapeDtypeStruct((full, layers * width), f32),
        ),
        in_specs=[in_smem] * 4 + [in_vmem] * 2 + [anywhere, in_vmem],
        out_specs=(in_vmem, in_vmem),
        scratch_shapes=[
            pltpu.SMEM((tri,), jnp.int32),
            pltpu.VMEM((occ_count, rows, full), amps.dtype),
            pltpu.VMEM((occ_count * rows, layers * width), f32),
            pltpu.VMEM((occ_count * rows, layers * width), f32),
            pltpu.VMEM((layers, rows, width), f32),
            dma((occ_count,)),
        ],
        compiler_params=pltpu.CompilerParams(vmem_limit_bytes=48 << 20),
        name="contract_pairs",
    )(block_sizes, roots, triples_all, occ_gap, vir_gap[:, None], pair_gap[None, :], amps_all, vvvo_all)
    steps = bits_of(ring)
    levels = bits_of(vir)
    halves = [(layers, vir >> (level + 1), depth, width) for level in range(levels)]
    grad_share, density_all = pl.pallas_call(
        functools.partial(reduce_kernel, tri, vir, split),
        out_shape=(
            jax.ShapeDtypeStruct((BMAX, depth, width), f32),
            jax.ShapeDtypeStruct((own_rows, width), f32),
        ),
        in_specs=[in_vmem] * 2,
        out_specs=(in_vmem, in_vmem),
        scratch_shapes=[pltpu.VMEM(shape, f32) for shape in halves + halves]
        + [
            pltpu.VMEM((BMAX, depth, width), f32),
            pltpu.VMEM((steps, rows, width), f32),
            pltpu.VMEM((steps, rows, width), f32),
            dma((levels, layers, vir // 2)),
            dma((levels, layers, vir // 2)),
            dma((BMAX,)),
            dma((BMAX,)),
            dma((steps + 1,)),
            dma((steps + 1,)),
        ],
        compiler_params=pltpu.CompilerParams(
            collective_id=1, has_side_effects=True, vmem_limit_bytes=24 << 20
        ),
        name="reduce_sums",
    )(grad, density)
    return density_all, grad_share


def solution(mesh):
    return jax.shard_map(
        functools.partial(body, mesh.shape["tri"], mesh.shape["vir"]),
        mesh=mesh,
        in_specs=(
            P("tri", "vir", None),
            P("tri", "vir", None),
            P(),
            P("vir"),
            P(),
            P(),
            P(),
            P("tri", None),
        ),
        out_specs=(P("vir", None), P("tri", "vir", None)),
        check_vma=False,
    )
```

time: 350 us -> 102 us (0.29)
  waiting for transfers between devices: 191 us -> 0 us
  Pallas kernels: 0 us -> 93 us
  matrix products: 52.2 us -> 0 us
  other arithmetic: 46 us -> 0 us
  local copies, waits for them, and re-layouts: 35.5 us -> 8.07 us
  between operations: 13.8 us -> 0.68 us
  blocking collectives: 9.18 us -> 0 us
    all_gather x1 -> x0, waiting for transfers between devices: 97.6 us -> none  [body(): everything = lax.all_gather(amps, 'tri', axis=0, tiled=True)]
    pallas_call x0 -> x3, Pallas kernels: none -> 93 us  [the longest x1 52.9 us: body(): pl.pallas_call(functools.partial(gather_kernel, tri, vir, split), out_sha...]
    psum x1 -> x0, waiting for transfers between devices: 66.3 us -> none  [body(): density_all = lax.psum(density, 'tri') / float(tri_count * pair_count)]
    dot_general x24 -> x0, matrix products: 52.2 us -> none  [the longest x12 39.1 us: pair_terms(): jnp.einsum('rnw,rqnhe->hwe', left_rows, weighted, precision=lax.Precision...]
    reduce_scatter x1 -> x0, waiting for transfers between devices: 26.4 us -> none  [body(): lax.psum_scatter(grad_part, 'vir', scatter_dimension=1, tiled=True)]
    dynamic_slice x36 -> x0, local copies, waits for them, and re-layouts: 19.3 us -> none  [body(): lax.scan(accumulate, start_state, (chosen, pair_gaps, pair_live))]
    select_n x2 -> x0, other arithmetic: 15.4 us -> none  [body(): jnp.take(everything, row_ids.reshape(-1), axis=0)]
    reduce_sum x16 -> x0, other arithmetic: 13.5 us -> none  [the longest x12 9.7 us: pair_terms(): jnp.einsum('rnw,rqnhe->hwe', left_rows, weighted, precision=lax.Precision...]
  transfers between devices with their start and end apart: 3 -> 0, of which waited for: 3 -> 0; matrix products, arithmetic and copies ran while one was open for 3% -> 0% of each run, Pallas kernels for 0% -> 0%
where the time goes in v2:
time: 102 us
  Pallas kernels  93 us (91%)
  local copies, waits for them, and re-layouts  8.07 us (8%)
    pallas_call x1, Pallas kernels, body(): pl.pallas_call(functools.partial(gather_kernel, tri, vir, split), out_sha...  52.9 us
    pallas_call x1, Pallas kernels, body(): pl.pallas_call(functools.partial(reduce_kernel, tri, vir, split), out_sha...  26.7 us
    pallas_call x1, Pallas kernels, body(): pl.pallas_call(functools.partial(contract_kernel, split, tri), out_shape=...  13.3 us
    unnamed x15, local copies, waits for them, and re-layouts  6.68 us

profile of v2, /device:TPU:0, one launch (start us, length us, event | category | flops | bytes accessed | tf_op | source)
XLA Modules:
  0.0 101.7 jit_solution(16027842043445712995)
XLA Ops:
  0.6 0.8 copy.11
  1.4 0.6 reshape.7.triples
  2.0 0.8 copy.12.vir_gap
  2.8 52.9 %gather_rows.1 = (bf16[24,96,768]{2,1,0:T(8,128)(2,1)}, bf16[6,768,128]{2,1,0:T(8,128)(2,1)}, s32[2,1,24]{2,1,0:T(1,128)}) custom-call(bf16[3,192,768]{2,1,0:T(8,128)(2,1)} %amps.1, bf16[3,192,128]{2,1,0:T(8,128)(2,1)} %vvvo.1, s32[1,24]{1,0:T(1,128)} %reshape.7.triples), custom_call_target="tpu_custom_call" | custom-call | tf_op jit(solution)/shard_map/gather_rows/pallas_call | solution.py:444
  55.7 0.0 copy-start
  55.7 1.3 %copy-done = bf16[6,768,128]{2,1,0:T(8,128)(2,1)S(1)} copy-done((bf16[6,768,128]{2,1,0:T(8,128)(2,1)S(1)}, bf16[6,768,128]{2,1,0:T(8,128)(2,1)}, u32[]{:S(2)}) %copy-start) | copy-done | bytes 1179672
  57.0 0.0 copy-start.1
  57.0 0.7 copy-done.1
  57.7 0.0 copy-start.2
  57.7 0.7 copy-done.2
  58.3 0.0 copy-start.3
  58.3 0.7 copy-done.3
  59.0 0.0 copy-start.4
  59.0 0.7 copy-done.4
  59.6 0.0 copy-start.5
  59.6 0.7 copy-done.5
  60.3 13.3 %contract_pairs.1 = (f32[96,128]{1,0:T(8,128)S(1)}, f32[768,768]{1,0:T(8,128)S(1)}) custom-call(s32[8]{0:T(128)S(1)} %copy-done.2, s32[8]{0:T(128)S(1)} %copy-done.3, s32[2,1,24]{2,1,0:T(1,128)S(1)} %copy-done.1, f32[16]{0:T(128)S(1)} %copy-done.4, f32[192,1]{1,0:T(8,128)S(1)} %copy.12.vir_gap, f32[1,128]{1,0:T(1,128)S(1)} %bitcast.2, ...), custom_call_target="tpu_custom_call" | custom-call | tf_op jit(solution)/shard_map/contract_pairs/pallas_call | solution.py:467
  73.6 26.7 %reduce_sums.1 = (f32[3,192,128]{2,1,0:T(8,128)S(1)}, f32[192,128]{1,0:T(8,128)S(1)}) custom-call(f32[768,768]{1,0:T(8,128)S(1)} %get-tuple-element.12.grad, f32[96,128]{1,0:T(8,128)S(1)} %get-tuple-element.13.dens), custom_call_target="tpu_custom_call" | custom-call | tf_op jit(solution)/shard_map/reduce_sums/pallas_call | solution.py:489
  100.4 0.6 copy.15
  101.0 0.7 copy.16
Async XLA Ops:
  55.7 1.3 %copy-start = (bf16[6,768,128]{2,1,0:T(8,128)(2,1)S(1)}, bf16[6,768,128]{2,1,0:T(8,128)(2,1)}, u32[]{:S(2)}) copy-start(bf16[6,768,128]{2,1,0:T(8,128)(2,1)} %get-tuple-element.11.vvvo) | copy-start | bytes 3538948
  57.0 0.7 copy-start.1
  57.7 0.7 copy-start.2
  58.3 0.7 copy-start.3
  59.0 0.7 copy-start.4
  59.6 0.7 copy-start.5

commit v3 on v2

--- a/solution.py
+++ b/solution.py
@@ -108,18 +108,61 @@
             device_id_type=MESH,
         )
 
+    square = split == 2 and ring == 4
+
+    def flipped(number, axis):
+        far = 1 << axis
+        return number + far * (1 - 2 * ((number // far) % 2))
+
+    def block(e, holder, slot):
+        return amps_all.at[((part + e) % split * ring + holder) * BMAX + slot]
+
+    def to_near(e, axis, slot, holder):
+        return pltpu.make_async_remote_copy(
+            src_ref=amps.at[slot, part_rows(part), :] if e == 0 else block(e, member, slot),
+            dst_ref=block(e, holder, slot),
+            send_sem=send_sem.at[e, axis, 0, slot],
+            recv_sem=recv_sem.at[e, axis, 0, slot],
+            device_id=(part * ring + flipped(member, axis), v),
+            device_id_type=MESH,
+        )
+
+    def way_on(e, slot):
+        return 1 if (e, slot) == (0, 0) else 0
+
+    def to_far(e, slot, holder):
+        axis = way_on(e, slot)
+        return pltpu.make_async_remote_copy(
+            src_ref=block(e, holder, slot),
+            dst_ref=block(e, holder, slot),
+            send_sem=send_sem.at[e, 0, 1, slot],
+            recv_sem=recv_sem.at[e, 0, 1, slot],
+            device_id=(part * ring + flipped(member, axis), v),
+            device_id_type=MESH,
+        )
+
+    def pass_on(e, slot):
+        axis = 1 - way_on(e, slot)
+        to_near(e, axis, slot, flipped(member, axis)).wait_recv()
+        to_far(e, slot, flipped(member, axis)).start()
+
     across = []
     if split == 2:
         across = [
             to_partner(0, triples, triples_all.at[1]),
             to_partner(1, vvvo, integral_place(1, v)),
         ]
+    if split == 2:
+        for slot in range(BMAX):
+            partner_copy(slot, t).start()
+    for slot in range(BMAX):
+        if square:
+            for axis in (1, 0):
+                to_near(0, axis, slot, member).start()
+        else:
+            start_ring(0, 0, slot)
     for copy in across:
         copy.start()
-    for slot in range(BMAX):
-        start_ring(0, 0, slot)
-        if split == 2:
-            partner_copy(slot, t).start()
     for hop in range(1, vir):
         integral_copy(0, hop, v).start()
     own = [
@@ -132,7 +175,26 @@
     for copy in own:
         copy.start()
 
-    if split == 2:
+    if square:
+        order = [(6 + 4 * slot, 0, slot) for slot in range(BMAX)]
+        order += [(8 * (slot + 1), 1, slot) for slot in range(BMAX)]
+        order += [(13 + 8 * slot, 2, slot) for slot in range(BMAX)]
+        order += [(25, 3, 0)]
+        for _, kind, slot in sorted(order):
+            if kind == 0:
+                pass_on(0, slot)
+            elif kind == 1:
+                partner_copy(slot, other_owner).wait_recv()
+                for axis in (1, 0):
+                    to_near(1, axis, slot, member).start()
+            elif kind == 2:
+                pass_on(1, slot)
+            else:
+                for copy in across:
+                    copy.wait_recv()
+                for hop in range(1, vir):
+                    integral_copy(1, hop, v).start()
+    elif split == 2:
         for copy in across:
             copy.wait_recv()
         for hop in range(1, vir):
@@ -155,6 +217,14 @@
 
     for e in range(split):
         for slot in range(BMAX):
+            if square:
+                axis = way_on(e, slot)
+                to_near(e, axis, slot, flipped(member, axis)).wait_recv()
+                to_far(e, slot, ring - 1 - member).wait_recv()
+                to_far(e, slot, flipped(member, 1 - axis)).wait_send()
+                for axis in range(2):
+                    to_near(e, axis, slot, member).wait_send()
+                continue
             for way in range(2):
                 ring_copy(e, way, ring - 2, slot, arriving=True).wait_recv()
                 ring_copy(e, way, 0, slot, first=e == 0).wait_send()
@@ -165,7 +235,8 @@
                     ring_copy(e, way, step, slot).wait_send()
             return carry
 
-        lax.fori_loop(1, ring - 1, drain, 0)
+        if not square:
+            lax.fori_loop(1, ring - 1, drain, 0)
         for hop in range(1, vir):
             integral_copy(e, hop, (v + vir - hop) % vir).wait_recv()
             integral_copy(e, hop, v).wait_send()
@@ -179,10 +250,26 @@
 
 
 def contract_kernel(
-    split, tri, sizes, roots, triples, occ_gap, vir_gap, pair_gap, amps, vvvo,
-    density, grad, offsets, rows_in, proj, weights, base, row_sem,
+    split, tri, sizes_in, roots_in, occ_gap_in, triples_in, pair_gap_in, vir_gap_in, vvvo_in, amps,
+    density, grad, sizes, roots, occ_gap, triples, pair_gap, vir_gap, vvvo,
+    offsets, rows_in, proj, weights, base, row_sem, load_sem,
 ):
-    pairs = triples.shape[2] // 2
+    loads = [
+        pltpu.make_async_copy(source, landing, load_sem.at[index])
+        for index, (source, landing) in enumerate(
+            [
+                (sizes_in, sizes), (roots_in, roots), (occ_gap_in, occ_gap), (triples_in, triples),
+                (pair_gap_in, pair_gap), (vir_gap_in, vir_gap), (vvvo_in, vvvo),
+            ]
+        )
+    ]
+    for load in loads:
+        load.start()
+    density[...] = jnp.zeros_like(density)
+    weights[...] = jnp.zeros_like(weights)
+    for load in loads[:6]:
+        load.wait()
+    pairs = triples.shape[2]
     occ_count = occ_gap.shape[0]
     rows = amps.shape[1]
     width = vvvo.shape[2]
@@ -210,13 +297,15 @@
         )
 
     owned = [find((t + e * ring) % tri) for e in range(split)]
-    outer = vir_gap[pl.ds(pl.multiple_of((t // ring) * rows, 8), rows), :] + pair_gap[...]
+    all_rows = vir_gap.shape[1]
+    own_place = lax.broadcasted_iota(jnp.int32, (rows, all_rows), 0) + (t // ring) * rows
+    picked = lax.broadcasted_iota(jnp.int32, (rows, all_rows), 1) == own_place
+    outer = jnp.sum(jnp.where(picked, vir_gap[...], 0.0), axis=1, keepdims=True) + pair_gap[...]
     for e in range(split):
         for k in range(BMAX):
             own_gap = occ_gap[jnp.minimum(offsets[owned[e]] + k, occ_count - 1)]
             base[e * BMAX + k] = outer + own_gap
-    density[...] = jnp.zeros_like(density)
-    weights[...] = jnp.zeros_like(weights)
+    loads[6].wait()
     table = jnp.concatenate([vvvo[layer] for layer in range(layers)], axis=1)
     group = 768 // rows
     span = group * rows
@@ -238,7 +327,7 @@
     scale = 1.0 / float(tri * pairs)
 
     def one_pair(e, q):
-        left, right = triples[e, 0, 2 * q], triples[e, 0, 2 * q + 1]
+        left, right = triples[e, 0, q], triples[e, 1, q]
         left_first, right_first = offsets[left], offsets[right]
         for count in range(1, BMAX + 1):
 
@@ -438,7 +527,7 @@
     layers = split * BMAX
     anywhere = pl.BlockSpec(memory_space=pl.ANY)
     in_vmem = pl.BlockSpec(memory_space=pltpu.VMEM)
-    in_smem = pl.BlockSpec(memory_space=pltpu.SMEM)
+    in_hbm = pl.BlockSpec(memory_space=pltpu.HBM)
     f32 = jnp.float32
     dma = pltpu.SemaphoreType.DMA
     amps_all, vvvo_all, triples_all = pl.pallas_call(
@@ -446,7 +535,7 @@
         out_shape=(
             jax.ShapeDtypeStruct((tri * BMAX, rows, full), amps.dtype),
             jax.ShapeDtypeStruct((layers, full, width), vvvo.dtype),
-            jax.ShapeDtypeStruct((split, 1, 2 * pairs), triples.dtype),
+            jax.ShapeDtypeStruct((split, 2, pairs), triples.dtype),
         ),
         in_specs=[anywhere] * 3,
         out_specs=(anywhere,) * 3,
@@ -463,26 +552,34 @@
         ],
         compiler_params=pltpu.CompilerParams(collective_id=0, has_side_effects=True),
         name="gather_rows",
-    )(amps, vvvo, triples.reshape(1, 2 * pairs))
+    )(amps, vvvo, triples.T)
     density, grad = pl.pallas_call(
         functools.partial(contract_kernel, split, tri),
         out_shape=(
             jax.ShapeDtypeStruct((rows, width), f32),
             jax.ShapeDtypeStruct((full, layers * width), f32),
         ),
-        in_specs=[in_smem] * 4 + [in_vmem] * 2 + [anywhere, in_vmem],
+        in_specs=[in_hbm] * 8,
         out_specs=(in_vmem, in_vmem),
         scratch_shapes=[
+            pltpu.SMEM((tri,), jnp.int32),
+            pltpu.SMEM((tri,), jnp.int32),
+            pltpu.SMEM((occ_count,), f32),
+            pltpu.SMEM((split, 2, pairs), jnp.int32),
+            pltpu.VMEM((1, width), f32),
+            pltpu.VMEM((1, own_rows), f32),
+            pltpu.VMEM((layers, full, width), vvvo.dtype),
             pltpu.SMEM((tri,), jnp.int32),
             pltpu.VMEM((occ_count, rows, full), amps.dtype),
             pltpu.VMEM((occ_count * rows, layers * width), f32),
             pltpu.VMEM((occ_count * rows, layers * width), f32),
             pltpu.VMEM((layers, rows, width), f32),
             dma((occ_count,)),
+            dma((7,)),
         ],
         compiler_params=pltpu.CompilerParams(vmem_limit_bytes=48 << 20),
         name="contract_pairs",
-    )(block_sizes, roots, triples_all, occ_gap, vir_gap[:, None], pair_gap[None, :], amps_all, vvvo_all)
+    )(block_sizes, roots, occ_gap, triples_all, pair_gap[None, :], vir_gap[None, :], vvvo_all, amps_all)
     steps = bits_of(ring)
     levels = bits_of(vir)
     halves = [(layers, vir >> (level + 1), depth, width) for level in range(levels)]

time: 102 us -> 104 us (1.020)
  Pallas kernels: 93 us -> 96.5 us
  local copies, waits for them, and re-layouts: 8.07 us -> 6.59 us
    pallas_call x1, Pallas kernels: 52.9 us -> 56.9 us  [body(): pl.pallas_call(functools.partial(gather_kernel, tri, vir, split), out_sha...]
    pallas_call x1, Pallas kernels: 26.7 us -> 24.1 us  [body(): pl.pallas_call(functools.partial(reduce_kernel, tri, vir, split), out_sha...]
    pallas_call x1, Pallas kernels: 13.3 us -> 15.5 us  [body(): pl.pallas_call(functools.partial(contract_kernel, split, tri), out_shape=...]
    unnamed x15 -> x16, local copies, waits for them, and re-layouts: 6.68 us -> 6.59 us
where the time goes in v3:
time: 104 us
  Pallas kernels  96.5 us (93%)
  local copies, waits for them, and re-layouts  6.59 us (6%)
    pallas_call x1, Pallas kernels, body(): pl.pallas_call(functools.partial(gather_kernel, tri, vir, split), out_sha...  56.9 us
    pallas_call x1, Pallas kernels, body(): pl.pallas_call(functools.partial(reduce_kernel, tri, vir, split), out_sha...  24.1 us
    pallas_call x1, Pallas kernels, body(): pl.pallas_call(functools.partial(contract_kernel, split, tri), out_shape=...  15.5 us
    unnamed x16, local copies, waits for them, and re-layouts  6.59 us

profile of v3, /device:TPU:0, one launch (start us, length us, event | category | flops | bytes accessed | tf_op | source)
XLA Modules:
  0.0 103.8 jit_solution(10136341120805655073)
XLA Ops:
  0.6 56.9 %gather_rows.1 = (bf16[24,96,768]{2,1,0:T(8,128)(2,1)}, bf16[6,768,128]{2,1,0:T(8,128)(2,1)}, s32[2,2,12]{2,1,0:T(2,128)}) custom-call(bf16[3,192,768]{2,1,0:T(8,128)(2,1)} %amps.1, bf16[3,192,128]{2,1,0:T(8,128)(2,1)} %vvvo.1, s32[2,12]{1,0:T(2,128)} %bitcast.5), custom_call_target="tpu_custom_call" | custom-call | tf_op jit(solution)/shard_map/gather_rows/pallas_call | solution.py:533
  57.6 0.0 copy-start
  57.6 1.3 %copy-done = bf16[6,768,128]{2,1,0:T(8,128)(2,1)S(1)} copy-done((bf16[6,768,128]{2,1,0:T(8,128)(2,1)S(1)}, bf16[6,768,128]{2,1,0:T(8,128)(2,1)}, u32[]{:S(2)}) %copy-start) | copy-done | bytes 1179672
  58.8 0.0 copy-start.1
  58.8 0.7 copy-done.1
  59.5 0.0 copy-start.2
  59.5 0.7 copy-done.2
  60.2 0.0 copy-start.3
  60.2 0.7 copy-done.3
  60.8 0.0 copy-start.4
  60.8 0.7 copy-done.4
  61.5 0.0 copy-start.5
  61.5 0.7 copy-done.5
  62.1 0.0 copy-start.6
  62.2 0.7 copy-done.6
  62.8 15.5 %contract_pairs.1 = (f32[96,128]{1,0:T(8,128)S(1)}, f32[768,768]{1,0:T(8,128)S(1)}) custom-call(s32[8]{0:T(128)S(1)} %copy-done.3, s32[8]{0:T(128)S(1)} %copy-done.4, f32[16]{0:T(128)S(1)} %copy-done.5, s32[2,2,12]{2,1,0:T(2,128)S(1)} %copy-done.1, f32[1,128]{1,0:T(1,128)S(1)} %bitcast.4, f32[1,192]{1,0:T(1,128)S(1)} %bitcast.3, ...), custom_call_target="tpu_custom_call" | custom-call | tf_op jit(solution)/shard_map/contract_pairs/pallas_call | solution.py:556
  78.3 24.1 %reduce_sums.1 = (f32[3,192,128]{2,1,0:T(8,128)S(1)}, f32[192,128]{1,0:T(8,128)S(1)}) custom-call(f32[768,768]{1,0:T(8,128)S(1)} %get-tuple-element.12.grad, f32[96,128]{1,0:T(8,128)S(1)} %get-tuple-element.13.dens), custom_call_target="tpu_custom_call" | custom-call | tf_op jit(solution)/shard_map/reduce_sums/pallas_call | solution.py:586
  102.4 0.6 copy.12
  103.1 0.7 copy.13
Async XLA Ops:
  57.6 1.3 %copy-start = (bf16[6,768,128]{2,1,0:T(8,128)(2,1)S(1)}, bf16[6,768,128]{2,1,0:T(8,128)(2,1)}, u32[]{:S(2)}) copy-start(bf16[6,768,128]{2,1,0:T(8,128)(2,1)} %get-tuple-element.10.vvvo_in) | copy-start | bytes 3538948
  58.8 0.7 copy-start.1
  59.5 0.7 copy-start.2
  60.2 0.7 copy-start.3
  60.8 0.7 copy-start.4
  61.5 0.7 copy-start.5
  62.1 0.7 copy-start.6

commit v4 on v3

--- a/solution.py
+++ b/solution.py
@@ -152,17 +152,18 @@
             to_partner(0, triples, triples_all.at[1]),
             to_partner(1, vvvo, integral_place(1, v)),
         ]
-    if split == 2:
+    if square:
+        partner_copy(0, t).start()
+        to_near(0, 1, 0, member).start()
         for slot in range(BMAX):
-            partner_copy(slot, t).start()
-    for slot in range(BMAX):
-        if square:
-            for axis in (1, 0):
-                to_near(0, axis, slot, member).start()
-        else:
+            to_near(0, 0, slot, member).start()
+    else:
+        for slot in range(BMAX):
+            if split == 2:
+                partner_copy(slot, t).start()
             start_ring(0, 0, slot)
-    for copy in across:
-        copy.start()
+        for copy in across:
+            copy.start()
     for hop in range(1, vir):
         integral_copy(0, hop, v).start()
     own = [
@@ -176,10 +177,10 @@
         copy.start()
 
     if square:
-        order = [(6 + 4 * slot, 0, slot) for slot in range(BMAX)]
-        order += [(8 * (slot + 1), 1, slot) for slot in range(BMAX)]
-        order += [(13 + 8 * slot, 2, slot) for slot in range(BMAX)]
-        order += [(25, 3, 0)]
+        order = [(6, 0, 0), (12, 0, 1), (19, 0, 2)]
+        order += [(8 + 7 * slot, 1, slot) for slot in range(BMAX)]
+        order += [(14, 2, 0), (22, 2, 1), (28, 2, 2), (30, 4, 0)]
+        order += [(7, 3, 0), (13, 3, 1), (20, 3, 2)]
         for _, kind, slot in sorted(order):
             if kind == 0:
                 pass_on(0, slot)
@@ -189,6 +190,14 @@
                     to_near(1, axis, slot, member).start()
             elif kind == 2:
                 pass_on(1, slot)
+            elif kind == 3:
+                partner_copy(slot, t).wait_send()
+                if slot + 1 < BMAX:
+                    partner_copy(slot + 1, t).start()
+                    to_near(0, 1, slot + 1, member).start()
+                else:
+                    for copy in across:
+                        copy.start()
             else:
                 for copy in across:
                     copy.wait_recv()
@@ -243,8 +252,9 @@
     if split == 2:
         for copy in across:
             copy.wait_send()
-        for slot in range(BMAX):
-            partner_copy(slot, t).wait_send()
+        if not square:
+            for slot in range(BMAX):
+                partner_copy(slot, t).wait_send()
     for copy in own:
         copy.wait()
 
@@ -470,30 +480,33 @@
         for j in range(vir // 2):
             halving(0, chunk, j).start()
     density_copy(0).start()
-    for level in range(levels):
-        if level:
-            step = level - 1
-            if step < steps:
-                density_copy(step).wait_recv()
-                dens_sum[step] = (dens[...] if step == 0 else dens_sum[step - 1]) + dens_in[step]
-                if step + 1 < steps:
-                    density_copy(step + 1).start()
-        for chunk in chunks:
-            for j in range(vir >> (level + 1)):
-                halving(level, chunk, j).wait_recv()
-                kept = 2 * j + bit(v, level)
-                held = grad[slab(kept), lanes(chunk)] if level == 0 else sums[level - 1][chunk, kept]
-                sums[level][chunk, j] = held + came[level][chunk, j]
-            if level + 1 < levels:
-                for j in range(vir >> (level + 2)):
-                    halving(level + 1, chunk, j).start()
-            elif chunk >= BMAX:
-                partner_copy(chunk - BMAX).start()
-    for step in range(max(levels - 1, 0), steps):
+    def add_density(step):
         density_copy(step).wait_recv()
         dens_sum[step] = (dens[...] if step == 0 else dens_sum[step - 1]) + dens_in[step]
         if step + 1 < steps:
             density_copy(step + 1).start()
+
+    ahead = 2
+    for level in range(levels):
+        last = level + 1 == levels
+        for index, chunk in enumerate(chunks):
+            for j in range(vir >> (level + 1)):
+                halving(level, chunk, j).wait_recv()
+                if level and last and index + ahead < len(chunks):
+                    halving(level, chunks[index + ahead], j).start()
+                kept = 2 * j + bit(v, level)
+                held = grad[slab(kept), lanes(chunk)] if level == 0 else sums[level - 1][chunk, kept]
+                sums[level][chunk, j] = held + came[level][chunk, j]
+            if not last:
+                if level + 2 < levels or index < ahead:
+                    for j in range(vir >> (level + 2)):
+                        halving(level + 1, chunk, j).start()
+            elif chunk >= BMAX:
+                partner_copy(chunk - BMAX).start()
+            if level and index == BMAX - 1 and level - 1 < steps:
+                add_density(level - 1)
+    for step in range(max(levels - 1, 0), steps):
+        add_density(step)
     dens_out[pl.ds(pl.multiple_of(part * rows, 8), rows), :] = dens_sum[steps - 1]
     if split == 2:
         part_copy(part).start()
@@ -577,7 +590,7 @@
             dma((occ_count,)),
             dma((7,)),
         ],
-        compiler_params=pltpu.CompilerParams(vmem_limit_bytes=48 << 20),
+        compiler_params=pltpu.CompilerParams(vmem_limit_bytes=60 << 20),
         name="contract_pairs",
     )(block_sizes, roots, occ_gap, triples_all, pair_gap[None, :], vir_gap[None, :], vvvo_all, amps_all)
     steps = bits_of(ring)

time: 104 us -> 94.1 us (0.905)
  Pallas kernels: 96.5 us -> 89.2 us
  local copies, waits for them, and re-layouts: 6.59 us -> 3.81 us
    pallas_call x1, Pallas kernels: 56.9 us -> 49 us  [body(): pl.pallas_call(functools.partial(gather_kernel, tri, vir, split), out_sha...]
    unnamed x16 -> x6, local copies, waits for them, and re-layouts: 6.59 us -> 3.81 us
where the time goes in v4:
time: 94.1 us; the launch traced here: 93.6 us
  Pallas kernels  89.2 us (95%)
  local copies, waits for them, and re-layouts  3.81 us (4%)
    pallas_call x1, Pallas kernels, body(): pl.pallas_call(functools.partial(gather_kernel, tri, vir, split), out_sha...  49 us
    pallas_call x1, Pallas kernels, body(): pl.pallas_call(functools.partial(reduce_kernel, tri, vir, split), out_sha...  24.3 us
    pallas_call x1, Pallas kernels, body(): pl.pallas_call(functools.partial(contract_kernel, split, tri), out_shape=...  15.9 us
    unnamed x6, local copies, waits for them, and re-layouts  3.81 us

profile of v4, /device:TPU:0, one launch (start us, length us, event | category | flops | bytes accessed | tf_op | source)
XLA Modules:
  0.0 93.6 jit_solution(13326856187399712593)
XLA Ops:
  0.6 49.0 %gather_rows.1 = (bf16[24,96,768]{2,1,0:T(8,128)(2,1)}, bf16[6,768,128]{2,1,0:T(8,128)(2,1)}, s32[2,2,12]{2,1,0:T(2,128)}) custom-call(bf16[3,192,768]{2,1,0:T(8,128)(2,1)} %amps.1, bf16[3,192,128]{2,1,0:T(8,128)(2,1)} %vvvo.1, s32[2,12]{1,0:T(2,128)} %bitcast.3), custom_call_target="tpu_custom_call" | custom-call | tf_op jit(solution)/shard_map/gather_rows/pallas_call | solution.py:546
  49.6 15.9 %contract_pairs.1 = (f32[96,128]{1,0:T(8,128)}, f32[768,768]{1,0:T(8,128)}) custom-call(s32[8]{0:T(128)} %sizes_in.1, s32[8]{0:T(128)} %roots_in.1, f32[16]{0:T(128)} %occ_gap_in.1, s32[2,2,12]{2,1,0:T(2,128)} %get-tuple-element.9.triples_in, f32[1,128]{1,0:T(1,128)} %bitcast.5, f32[1,192]{1,0:T(1,128)} %bitcast.4, ...), custom_call_target="tpu_custom_call" | custom-call | tf_op jit(solution)/shard_map/contract_pairs/pallas_call | solution.py:569
  65.5 0.0 copy-start
  65.5 1.7 %copy-done = f32[768,768]{1,0:T(8,128)S(1)} copy-done((f32[768,768]{1,0:T(8,128)S(1)}, f32[768,768]{1,0:T(8,128)}, u32[]{:S(2)}) %copy-start) | copy-done | bytes 2359320
  67.2 0.0 copy-start.1
  67.2 0.8 copy-done.1
  68.0 24.3 %reduce_sums.1 = (f32[3,192,128]{2,1,0:T(8,128)S(1)}, f32[192,128]{1,0:T(8,128)S(1)}) custom-call(f32[768,768]{1,0:T(8,128)S(1)} %copy-done, f32[96,128]{1,0:T(8,128)S(1)} %copy-done.1), custom_call_target="tpu_custom_call" | custom-call | tf_op jit(solution)/shard_map/reduce_sums/pallas_call | solution.py:599
  92.3 0.6 copy.12
  92.9 0.7 copy.13
Async XLA Ops:
  65.5 1.7 %copy-start = (f32[768,768]{1,0:T(8,128)S(1)}, f32[768,768]{1,0:T(8,128)}, u32[]{:S(2)}) copy-start(f32[768,768]{1,0:T(8,128)} %get-tuple-element.12.grad) | copy-start | bytes 7077892
  67.2 0.8 copy-start.1
